TPU v7x, 32 devices: a whole 2x2x4 slice. The times are simulated.
32 devices in a mesh: hst: 8 (over z, x), local: 4 (over y, core).
Axes of the slice: x: 2, y: 2, z: 4, core: 2. Of those that a mesh axis runs over, the one named last changes fastest.
Arguments:
- patches: bfloat16 [32768, 768], P(('hst', 'local')), may hold values from -6 to 6
- w_in: bfloat16 [768, 3072], replicated, may hold values from -0.21875 to 0.21875
- b_in: float32 [3072], replicated, may hold values from -3 to 3
- w_out: bfloat16 [3072, 512], replicated, may hold values from -0.15625 to 0.15625
- b_out: float32 [512], replicated, may hold values from -3 to 3
- ema_sums: float32 [32768, 512], P(('hst', 'local')), may hold values from -12 to 12
- ema_counts: float32 [32768], P(('hst', 'local')), may hold values from 0.5 to 4
- code_ids: int32 [32768], P(('hst', 'local')), may hold values from 0 to 32767, as said below
Outputs:
- codebook: float32 [32768, 512], P(('hst', 'local'))
- new_counts: float32 [32768], P(('hst', 'local'))
- quantized: bfloat16 [32768, 512], P(('hst', 'local'))
Inputs may be any that keep to these rules, and one draw needn't show every extreme that they name: `code_ids`: in each aligned block of 1024 patches (the patches of one device), at most 64 ids lie in any one range [k * 1024, (k + 1) * 1024); one such range gets exactly 64 from every block.
All inputs are finite; a program needn't handle non-finite values.
Results may differ from a plain program's by a relative error of at most 0.002.
Values may be sent and summed in bfloat16 or wider, within the bound.
A program may use at most 64 MiB of HBM per device.

v0:
```python
import jax
import jax.numpy as jnp
from jax import lax
from jax.sharding import PartitionSpec as P

DECAY = 0.9


def per_device(patches, w_in, b_in, w_out, b_out, ema_sums, ema_counts, code_ids):
    host_count = lax.axis_size("hst")
    local_count = lax.axis_size("local")
    owner_count = host_count * local_count
    code_span = ema_sums.shape[0]
    latent_width = ema_sums.shape[1]
    row_count = patches.shape[0]
    capacity = max(2, 2 * row_count // owner_count)
    pre_act = jnp.dot(patches, w_in, preferred_element_type=jnp.float32) + b_in
    hidden = jnp.tanh(pre_act).astype(jnp.bfloat16)
    latents = (jnp.dot(hidden, w_out, preferred_element_type=jnp.float32) + b_out).astype(
        jnp.bfloat16
    )
    owner_of = code_ids // code_span
    members = (owner_of[:, None] == jnp.arange(owner_count)[None, :]).astype(jnp.int32)
    running = jnp.cumsum(members, axis=0)
    position = jnp.sum(running * members, axis=1) - 1
    slot_index = owner_of * capacity + position
    placing = jnp.arange(owner_count * capacity)[:, None] == slot_index[None, :]
    outgoing = jnp.dot(
        placing.astype(jnp.bfloat16), latents, preferred_element_type=jnp.float32
    ).astype(jnp.bfloat16)
    sent_ids = jnp.max(jnp.where(placing, code_ids[None, :], -1), axis=1)
    outgoing = outgoing.reshape(host_count, local_count, capacity, latent_width)
    sent_ids = sent_ids.reshape(host_count, local_count, capacity)
    halfway = (
        lax.all_to_all(outgoing, "hst", split_axis=0, concat_axis=0, tiled=True),
        lax.all_to_all(sent_ids, "hst", split_axis=0, concat_axis=0, tiled=True),
    )
    arrived, arrived_ids = (
        lax.all_to_all(halfway[0], "local", split_axis=1, concat_axis=1, tiled=True),
        lax.all_to_all(halfway[1], "local", split_axis=1, concat_axis=1, tiled=True),
    )
    arrived = arrived.reshape(owner_count * capacity, latent_width)
    arrived_ids = arrived_ids.reshape(owner_count * capacity)
    first_code = (lax.axis_index("hst") * local_count + lax.axis_index("local")) * code_span
    offset_code = arrived_ids - first_code
    chosen = (offset_code[:, None] == jnp.arange(code_span)[None, :]).astype(jnp.bfloat16)
    code_sums = lax.dot_general(
        chosen, arrived, (((0,), (0,)), ((), ())), preferred_element_type=jnp.float32
    )
    code_counts = jnp.sum(chosen, axis=0, dtype=jnp.float32)
    new_counts = DECAY * ema_counts + (1.0 - DECAY) * code_counts
    codebook = (DECAY * ema_sums + (1.0 - DECAY) * code_sums) / new_counts[:, None]
    replies = jnp.dot(
        chosen, codebook.astype(jnp.bfloat16), preferred_element_type=jnp.float32
    ).astype(jnp.bfloat16)
    replies = replies.reshape(host_count, local_count, capacity, latent_width)
    returned = lax.all_to_all(
        lax.all_to_all(replies, "hst", split_axis=0, concat_axis=0, tiled=True),
        "local",
        split_axis=1,
        concat_axis=1,
        tiled=True,
    )
    back_rows = returned.reshape(owner_count * capacity, latent_width)
    quantized = jnp.take(back_rows, slot_index, axis=0)
    return (codebook, new_counts, quantized)


def solution(mesh):
    in_specs = (
        P(("hst", "local"), None),
        P(),
        P(),
        P(),
        P(),
        P(("hst", "local"), None),
        P(("hst", "local")),
        P(("hst", "local")),
    )
    out_specs = (P(("hst", "local"), None), P(("hst", "local")), P(("hst", "local"), None))
    return jax.shard_map(
        per_device, mesh=mesh, in_specs=in_specs, out_specs=out_specs, check_vma=False
    )
```

profile of v0, /device:TPU:0, one launch (start us, length us, event | category | flops | bytes accessed | tf_op | source)
XLA Modules:
  0.0 233.3 jit_solution(15178667271600228671)
XLA Ops:
  0.6 0.0 copy-start
  0.6 0.8 add_select_fusion
  1.5 9.0 %reduce-window.6 = s32[32,8,128]{2,1,0:T(8,128)S(1)} reduce-window(s32[32,8,128]{2,1,0:T(8,128)S(1)} %fusion.16, s32[]{:T(128)} %constant.26.clone.1), window={size=1x1x128 pad=0_0x0_0x127_0}, to_apply=%region_0.1 | reduce-window | flops 4161536 | bytes 262148 | tf_op jit(solution)/shard_map/reduce-window
  10.5 0.1 slice.10
  10.6 0.1 copy.34
  10.8 0.1 copy.35
  10.9 0.1 broadcast_add_fusion
  11.0 0.7 compare_and_fusion
  11.7 1.9 select_reduce_fusion
  13.6 0.1 reshape.56
  13.7 0.7 reshape.70
  14.4 7.3 %all-to-all-start = ((s32[8,1,256]{2,1,0:T(1,128)}), s32[8,1,256]{2,1,0:T(1,128)S(1)}, u32[]{:S(2)}, u32[]{:S(2)}) async-start(s32[8,1,256]{2,1,0:T(1,128)} %reshape.70), calls=%async_computation | async-start | bytes 16384 | tf_op jit(solution)/shard_map/all_to_all | solution.py:36
  21.6 0.0 copy-done
  21.6 12.1 %add_convert_fusion = bf16[1024,512]{1,0:T(8,128)(2,1)} fusion(bf16[3072,512]{1,0:T(8,128)(2,1)S(1)} %copy-done, f32[3072]{0:T(1024)} %param.10, bf16[1024,768]{1,0:T(8,128)(2,1)} %param.8, bf16[768,3072]{1,0:T(8,128)(2,1)} %param.9, f32[512]{0:T(512)} %param.12), kind=kOutput, calls=%fused_computation.19 | convolution fusion | flops 8060403712 | bytes 10500096 | tf_op jit(solution)/shard_map/dot_general | solution.py:19
  33.7 4.9 %fusion.10 = bf16[2048,512]{1,0:T(8,128)(2,1)} fusion(bf16[1024,512]{1,0:T(8,128)(2,1)} %add_convert_fusion, s32[1024]{0:T(1024)S(1)} %get-tuple-element.4), kind=kOutput, calls=%fused_computation.16 | convolution fusion | flops 2150629376 | bytes 3149824 | tf_op jit(solution)/shard_map/dot_general | solution.py:28
  38.6 0.0 all-to-all-done
  38.6 6.0 %all-to-all-start.2 = ((bf16[8,4,64,512]{3,2,1,0:T(8,128)(2,1)}), bf16[8,4,64,512]{3,2,1,0:T(8,128)(2,1)}, u32[]{:S(2)}, u32[]{:S(2)}) async-start(bf16[8,4,64,512]{3,2,1,0:T(8,128)(2,1)} %bitcast.31), calls=%async_computation.2 | async-start | bytes 4194304 | tf_op jit(solution)/shard_map/all_to_all | solution.py:35
  44.6 0.5 broadcast.64
  45.1 0.7 reduce
  45.8 0.1 reshape.71
  45.9 0.7 reshape.72
  46.6 45.8 %all-to-all-done.2 = bf16[8,4,64,512]{3,2,1,0:T(8,128)(2,1)} async-done(((bf16[8,4,64,512]{3,2,1,0:T(8,128)(2,1)}), bf16[8,4,64,512]{3,2,1,0:T(8,128)(2,1)}, u32[]{:S(2)}, u32[]{:S(2)}) %all-to-all-start.2) | async-done | bytes 2097184 | tf_op jit(solution)/shard_map/all_to_all | solution.py:35
  92.4 3.2 %all-to-all-start.1 = ((s32[4,1,512]{2,1,0:T(1,128)}), s32[4,1,512]{2,1,0:T(1,128)S(1)}, u32[]{:S(2)}, u32[]{:S(2)}) async-start(s32[4,1,512]{2,1,0:T(1,128)} %reshape.72), calls=%async_computation.1 | async-start | bytes 16384 | tf_op jit(solution)/shard_map/all_to_all | solution.py:40
  95.6 3.1 %copy.38 = bf16[8,4,64,512]{3,2,0,1:T(8,128)(2,1)} copy(bf16[8,4,64,512]{3,2,1,0:T(8,128)(2,1)} %all-to-all-done.2) | data formatting | bytes 4194304 | tf_op jit(solution)/shard_map/all_to_all | solution.py:35
  98.8 0.0 copy-start.1
  98.8 0.6 all-to-all-done.1
  99.4 4.6 %all-to-all-start.3 = ((bf16[8,4,64,512]{3,2,0,1:T(8,128)(2,1)}), bf16[8,4,64,512]{3,2,0,1:T(8,128)(2,1)}, u32[]{:S(2)}, u32[]{:S(2)}) async-start(bf16[8,4,64,512]{3,2,0,1:T(8,128)(2,1)} %copy.38), calls=%async_computation.3 | async-start | bytes 4194304 | tf_op jit(solution)/shard_map/all_to_all | solution.py:39
  104.1 0.7 reduce.1
  104.7 0.1 reshape.73
  104.8 0.1 sub.27
  104.9 1.0 convert_reduce_fusion
  105.9 0.0 copy-done.1
  105.9 0.0 copy-start.2
  105.9 23.7 %all-to-all-done.3 = bf16[8,4,64,512]{3,2,0,1:T(8,128)(2,1)} async-done(((bf16[8,4,64,512]{3,2,0,1:T(8,128)(2,1)}), bf16[8,4,64,512]{3,2,0,1:T(8,128)(2,1)}, u32[]{:S(2)}, u32[]{:S(2)}) %all-to-all-start.3) | async-done | bytes 2097184 | tf_op jit(solution)/shard_map/all_to_all | solution.py:39
  129.6 0.0 copy-start.3
  129.6 1.9 copy.39
  131.5 0.0 copy-done.2
  131.6 0.3 copy-done.3
  131.9 3.0 %add_divide_fusion = f32[1024,512]{1,0:T(8,128)S(1)} fusion(f32[1024,512]{1,0:T(8,128)S(1)} %copy-done.3, bf16[2048,512]{1,0:T(8,128)(2,1)S(1)} %bitcast.32, s32[2048]{0:T(1024)S(1)} %sub.27, f32[1024]{0:T(1024)S(1)} %multiply_add_fusion), kind=kOutput, calls=%fused_computation.18 | convolution fusion | flops 2151677952 | bytes 6303744 | tf_op jit(solution)/shard_map/dot_general | solution.py:47
  134.9 0.0 copy-start.4
  134.9 2.6 %fusion.9 = bf16[2048,512]{1,0:T(8,128)(2,1)S(1)} fusion(s32[2048]{0:T(1024)S(1)} %sub.27, f32[1024,512]{1,0:T(8,128)S(1)} %add_divide_fusion), kind=kOutput, calls=%fused_computation.15 | convolution fusion | flops 2151153664 | bytes 4202496 | tf_op jit(solution)/shard_map/dot_general | solution.py:53
  137.5 0.0 copy-done.4
  137.5 51.6 %all_to_all.30 = bf16[8,4,64,512]{3,2,1,0:T(8,128)(2,1)S(1)} all-to-all(bf16[8,4,64,512]{3,2,1,0:T(8,128)(2,1)S(1)} %bitcast.33), channel_id=1, replica_groups=mesh['hst'=8,'local'=4] {'hst'}, dimensions={0} | all-to-all | bytes 4194304 | tf_op jit(solution)/shard_map/all_to_all | solution.py:58
  189.1 1.5 copy.40
  190.6 4.4 %all-to-all-start.5 = ((bf16[8,4,64,512]{3,2,0,1:T(8,128)(2,1)}), bf16[8,4,64,512]{3,2,0,1:T(8,128)(2,1)}, u32[]{:S(2)}, u32[]{:S(2)}) async-start(bf16[8,4,64,512]{3,2,0,1:T(8,128)(2,1)} %copy.40), calls=%async_computation.5 | async-start | bytes 4194304 | tf_op jit(solution)/shard_map/all_to_all | solution.py:57
  195.1 25.7 %all-to-all-done.5 = bf16[8,4,64,512]{3,2,0,1:T(8,128)(2,1)} async-done(((bf16[8,4,64,512]{3,2,0,1:T(8,128)(2,1)}), bf16[8,4,64,512]{3,2,0,1:T(8,128)(2,1)}, u32[]{:S(2)}, u32[]{:S(2)}) %all-to-all-start.5) | async-done | bytes 2097184 | tf_op jit(solution)/shard_map/all_to_all | solution.py:57
  220.8 3.1 %copy.41 = bf16[8,4,64,512]{3,2,1,0:T(8,128)(2,1)} copy(bf16[8,4,64,512]{3,2,0,1:T(8,128)(2,1)} %all-to-all-done.5) | data formatting | bytes 4194304 | tf_op jit(solution)/shard_map/all_to_all | solution.py:57
  223.9 7.0 %gather_fusion = bf16[1024,512]{1,0:T(8,128)(2,1)} fusion(bf16[2048,512]{1,0:T(8,128)(2,1)} %bitcast.30, s32[1024]{0:T(1024)S(1)} %fusion.19), kind=kCustom, calls=%fused_computation | custom fusion | bytes 2101248 | tf_op jit(solution)/shard_map/jit(_take)/gather | solution.py:65
  230.9 2.4 %broadcast_select_fusion = bf16[1024,512]{1,0:T(8,128)(2,1)} fusion(bf16[1024,512]{1,0:T(8,128)(2,1)} %gather_fusion, pred[1024]{0:T(1024)(128)(4,1)S(1)} %get-tuple-element.3), kind=kLoop, calls=%fused_computation.21 | loop fusion | flops 524288 | bytes 2098176 | tf_op jit(solution)/shard_map/jit(_take)/select_n | solution.py:65
  (9 shorter events, 0.1 us)
Async XLA Ops:
  0.6 21.0 %copy-start = (bf16[3072,512]{1,0:T(8,128)(2,1)S(1)}, bf16[3072,512]{1,0:T(8,128)(2,1)}, u32[]{:S(2)}) copy-start(bf16[3072,512]{1,0:T(8,128)(2,1)} %param.11) | copy-start | bytes 9437188
  14.4 24.2 %all-to-all-start = ((s32[8,1,256]{2,1,0:T(1,128)}), s32[8,1,256]{2,1,0:T(1,128)S(1)}, u32[]{:S(2)}, u32[]{:S(2)}) async-start(s32[8,1,256]{2,1,0:T(1,128)} %reshape.70), calls=%async_computation | async-start | bytes 16384 | tf_op jit(solution)/shard_map/all_to_all | solution.py:36
  38.6 53.8 %all-to-all-start.2 = ((bf16[8,4,64,512]{3,2,1,0:T(8,128)(2,1)}), bf16[8,4,64,512]{3,2,1,0:T(8,128)(2,1)}, u32[]{:S(2)}, u32[]{:S(2)}) async-start(bf16[8,4,64,512]{3,2,1,0:T(8,128)(2,1)} %bitcast.31), calls=%async_computation.2 | async-start | bytes 4194304 | tf_op jit(solution)/shard_map/all_to_all | solution.py:35
  92.4 7.0 %all-to-all-start.1 = ((s32[4,1,512]{2,1,0:T(1,128)}), s32[4,1,512]{2,1,0:T(1,128)S(1)}, u32[]{:S(2)}, u32[]{:S(2)}) async-start(s32[4,1,512]{2,1,0:T(1,128)} %reshape.72), calls=%async_computation.1 | async-start | bytes 16384 | tf_op jit(solution)/shard_map/all_to_all | solution.py:40
  98.8 7.1 %copy-start.1 = (f32[1024]{0:T(1024)S(1)}, f32[1024]{0:T(1024)}, u32[]{:S(2)}) copy-start(f32[1024]{0:T(1024)} %param.14) | copy-start | bytes 12292
  99.4 30.2 %all-to-all-start.3 = ((bf16[8,4,64,512]{3,2,0,1:T(8,128)(2,1)}), bf16[8,4,64,512]{3,2,0,1:T(8,128)(2,1)}, u32[]{:S(2)}, u32[]{:S(2)}) async-start(bf16[8,4,64,512]{3,2,0,1:T(8,128)(2,1)} %copy.38), calls=%async_computation.3 | async-start | bytes 4194304 | tf_op jit(solution)/shard_map/all_to_all | solution.py:39
  105.9 25.6 %copy-start.2 = (f32[1024]{0:T(1024)}, f32[1024]{0:T(1024)S(1)}, u32[]{:S(2)}) copy-start(f32[1024]{0:T(1024)S(1)} %multiply_add_fusion) | copy-start | bytes 12292
  129.6 2.2 copy-start.3
  134.9 2.6 %copy-start.4 = (f32[1024,512]{1,0:T(8,128)}, f32[1024,512]{1,0:T(8,128)S(1)}, u32[]{:S(2)}) copy-start(f32[1024,512]{1,0:T(8,128)S(1)} %add_divide_fusion) | copy-start | bytes 6291460
  190.6 30.2 %all-to-all-start.5 = ((bf16[8,4,64,512]{3,2,0,1:T(8,128)(2,1)}), bf16[8,4,64,512]{3,2,0,1:T(8,128)(2,1)}, u32[]{:S(2)}, u32[]{:S(2)}) async-start(bf16[8,4,64,512]{3,2,0,1:T(8,128)(2,1)} %copy.40), calls=%async_computation.5 | async-start | bytes 4194304 | tf_op jit(solution)/shard_map/all_to_all | solution.py:57
where the time goes:
time: 234 us; the launch traced here: 233 us
  waiting for transfers between devices  95.9 us (41%)
  blocking collectives  51.6 us (22%)
  starting transfers between devices  25.6 us (11%)
  matrix products  22.6 us (10%)
  local copies, waits for them, and re-layouts  19.5 us (8%)
  other arithmetic  17.4 us (7%)
    all_to_all x1, blocking collectives, per_device(): lax.all_to_all(replies, 'hst', split_axis=0, concat_axis=0, tiled=True)  51.6 us
    all_to_all x1, waiting for transfers between devices, per_device(): lax.all_to_all(outgoing, 'hst', split_axis=0, concat_axis=0, tiled=True)  45.8 us
    all_to_all x1, waiting for transfers between devices, per_device(): lax.all_to_all(lax.all_to_all(replies, 'hst', split_axis=0, concat_axis=0...  25.7 us
    all_to_all x1, waiting for transfers between devices, per_device(): lax.all_to_all(halfway[0], 'local', split_axis=1, concat_axis=1, tiled=True)  23.7 us
    dot_general x1, matrix products, per_device(): jnp.dot(hidden, w_out, preferred_element_type=jnp.float32) + b_out  12.1 us
    another operation x3, other arithmetic  9.15 us
    all_to_all x1, starting transfers between devices, per_device(): lax.all_to_all(sent_ids, 'hst', split_axis=0, concat_axis=0, tiled=True)  7.25 us
    gather x1, local copies, waits for them, and re-layouts, per_device(): quantized = jnp.take(back_rows, slot_index, axis=0)  6.98 us
  transfers between devices with their start and end apart: 5, of which 4 were waited for; matrix products, arithmetic and copies ran while one was open for 10% of the time, Pallas kernels for 0%

commit v1 on v0

--- a/solution.py
+++ b/solution.py
@@ -1,12 +1,290 @@
+import functools
+
 import jax
 import jax.numpy as jnp
 from jax import lax
+from jax.experimental import pallas as pl
+from jax.experimental.pallas import tpu as pltpu
 from jax.sharding import PartitionSpec as P
 
 DECAY = 0.9
-
-
-def per_device(patches, w_in, b_in, w_out, b_out, ema_sums, ema_counts, code_ids):
+CHUNKS = 2
+MESH = pl.DeviceIdType.MESH
+F32 = jnp.float32
+BF16 = jnp.bfloat16
+
+
+def iota(shape, dim):
+    return lax.broadcasted_iota(jnp.int32, shape, dim)
+
+
+def to_column(row):
+    eye = iota((128, 128), 0) == iota((128, 128), 1)
+    return jnp.sum(jnp.where(eye, jnp.broadcast_to(row, (128, 128)), 0.0), axis=1, keepdims=True)
+
+
+def one_hot(mask):
+    return jnp.where(mask, 1.0, 0.0).astype(BF16)
+
+
+def dot_nt(a, b):
+    return lax.dot_general(a, b, (((1,), (1,)), ((), ())), preferred_element_type=F32)
+
+
+def kernel(
+    hosts, locals_, capacity,
+    patches_hbm, w_in_hbm, b_in, w_out_hbm, b_out, ema_hbm, counts_row, ids_row,
+    codebook, new_counts_row, quantized,
+    patches, w_in, w_out, ema, hidden, latents, placing, unplacing, chosen, chosen_t, scale,
+    ids_out, ids_in, out, arrived, replies, back,
+    load_sem, ids_send, ids_recv, send_a, recv_a, send_b, recv_b,
+):
+    owners = hosts * locals_
+    rows = patches.shape[0]
+    span, width = ema.shape
+    chunk = width // CHUNKS
+    slots = owners * capacity
+    group = 128 // capacity
+    my_host, my_local = lax.axis_index("hst"), lax.axis_index("local")
+    me = my_host * locals_ + my_local
+    stride = max(1, hosts // 2 - 1)
+
+    def peer(step):
+        host = lax.rem(my_host + stride * (lax.rem(step, hosts) + 1), hosts)
+        local = lax.rem(my_local + step // hosts + 1, locals_)
+        return host, local
+
+    def each_peer(body):
+        def run(step, carry):
+            host, local = peer(step)
+            body(host, local, host * locals_ + local)
+            return carry
+        lax.fori_loop(0, owners - 1, run, 0)
+
+    loads = [
+        pltpu.make_async_copy(src, dst, load_sem.at[at])
+        for at, (src, dst) in enumerate(
+            ((patches_hbm, patches), (w_in_hbm, w_in), (w_out_hbm, w_out), (ema_hbm, ema))
+        )
+    ]
+    for load in loads:
+        load.start()
+    barrier = pltpu.get_barrier_semaphore()
+    each_peer(
+        lambda host, local, rank: pl.semaphore_signal(
+            barrier, inc=1, device_id=(host, local), device_id_type=MESH
+        )
+    )
+
+    ids = ids_row[...]
+    owner = ids // span
+    members = iota((owners, rows), 0) == owner
+    before = one_hot(iota((rows, rows), 0) <= iota((rows, rows), 1))
+    running = jnp.dot(one_hot(members), before, preferred_element_type=F32)
+    position = jnp.sum(jnp.where(members, running, 0.0), axis=0, keepdims=True) - 1.0
+    position = position.astype(jnp.int32)
+    slot = owner * capacity + position
+    block = min(slots, 256)
+
+    def fill_placing(at, carry):
+        start = pl.multiple_of(at * block, block)
+        placing[pl.ds(start, block), :] = one_hot(iota((block, rows), 0) + start == slot)
+        return carry
+    lax.fori_loop(0, slots // block, fill_placing, 0)
+
+    code = ids - owner * span + 1
+    high, low = (code // 128).astype(F32), lax.rem(code, 128).astype(F32)
+    part = lax.rem(iota((owners * 8, rows), 0), 8)
+    value = jnp.where(part == 0, high, jnp.where(part == 1, low, 0.0))
+    sending = jnp.where(iota((owners * 8, rows), 0) // 8 == owner, value, 0.0).astype(BF16)
+    lane = position + capacity * lax.rem(me, group)
+    lanes = one_hot(iota((128, rows), 0) == lane)
+    ids_out[...] = dot_nt(sending, lanes).reshape(owners, 8, 128)
+    ids_in[pl.ds(me, 1)] = ids_out[pl.ds(me, 1)]
+
+    loads[0].wait()
+    loads[1].wait()
+    tile = 512
+
+    def first_layer(at, carry):
+        columns = pl.ds(pl.multiple_of(at * tile, tile), tile)
+        pre_act = jnp.dot(patches[...], w_in[:, columns], preferred_element_type=F32)
+        hidden[:, columns] = jnp.tanh(pre_act + b_in[:, columns]).astype(BF16)
+        return carry
+    lax.fori_loop(0, hidden.shape[1] // tile, first_layer, 0)
+    loads[2].wait()
+
+    def ids_copy(host, local, rank, slot_at):
+        return pltpu.make_async_remote_copy(
+            src_ref=ids_out.at[rank], dst_ref=ids_in.at[slot_at], send_sem=ids_send.at[rank],
+            recv_sem=ids_recv.at[slot_at], device_id=(host, local), device_id_type=MESH,
+        )
+
+    def rows_copy(at, source, target, send, recv, host, local, rank, slot_at):
+        return pltpu.make_async_remote_copy(
+            src_ref=source.at[at, rank], dst_ref=target.at[at, slot_at], send_sem=send.at[at, rank],
+            recv_sem=recv.at[at, slot_at], device_id=(host, local), device_id_type=MESH,
+        )
+
+    def send_latents(at):
+        columns = slice(at * chunk, (at + 1) * chunk)
+        latent = jnp.dot(hidden[...], w_out[:, columns], preferred_element_type=F32)
+        latents[...] = (latent + b_out[:, columns]).astype(BF16)
+
+        def pack(piece, carry):
+            some = pl.ds(pl.multiple_of(piece * block, block), block)
+            packed = jnp.dot(placing[some, :], latents[...], preferred_element_type=F32)
+            count = block // capacity
+            out[at, pl.ds(piece * count, count)] = packed.astype(BF16).reshape(
+                count, capacity, chunk
+            )
+            return carry
+        lax.fori_loop(0, slots // block, pack, 0)
+        if at == 0:
+            pl.semaphore_wait(barrier, owners - 1)
+            each_peer(lambda host, local, rank: ids_copy(host, local, rank, me).start())
+        each_peer(
+            lambda host, local, rank: rows_copy(
+                at, out, arrived, send_a, recv_a, host, local, rank, me
+            ).start()
+        )
+        arrived[at, pl.ds(me, 1)] = out[at, pl.ds(me, 1)]
+
+    for at in range(CHUNKS):
+        send_latents(at)
+
+    for at in range(rows // 128):
+        column = to_column(slot[:, at * 128:(at + 1) * 128].astype(F32)).astype(jnp.int32)
+        unplacing[at * 128:(at + 1) * 128, :] = one_hot(iota((128, slots), 1) == column)
+
+    each_peer(lambda host, local, rank: ids_copy(host, local, rank, rank).wait_recv())
+    for at in range(slots // 128):
+        codes = jnp.zeros((1, 128), F32)
+        for source in range(at * group, (at + 1) * group):
+            codes = codes + ids_in[source, 0:1, :] * 128.0 + ids_in[source, 1:2, :]
+        column = to_column(codes).astype(jnp.int32)
+        chosen[at * 128:(at + 1) * 128, :] = one_hot(iota((128, span), 1) + 1 == column)
+        chosen_t[:, at * 128:(at + 1) * 128] = one_hot(
+            iota((span, 128), 0) + 1 == codes.astype(jnp.int32)
+        )
+    counts = jnp.dot(jnp.ones((8, slots), BF16), chosen[...], preferred_element_type=F32)[0:1]
+    new_counts = DECAY * counts_row[...] + (1.0 - DECAY) * counts
+    new_counts_row[...] = new_counts
+    for at in range(span // 128):
+        scale[at * 128:(at + 1) * 128, :] = jnp.broadcast_to(
+            to_column(new_counts[:, at * 128:(at + 1) * 128]), (128, 128)
+        )
+    loads[3].wait()
+
+    for at in range(CHUNKS):
+        columns = slice(at * chunk, (at + 1) * chunk)
+        each_peer(
+            lambda host, local, rank: rows_copy(
+                at, out, arrived, send_a, recv_a, host, local, rank, rank
+            ).wait_recv()
+        )
+        sums = jnp.dot(
+            chosen_t[...], arrived[at].reshape(slots, chunk), preferred_element_type=F32
+        )
+        book = (DECAY * ema[:, columns] + (1.0 - DECAY) * sums) / scale[:, 0:1]
+        codebook[:, columns] = book
+        latents[...] = book.astype(BF16)
+
+        def reply(piece, carry):
+            some = pl.ds(pl.multiple_of(piece * block, block), block)
+            found = jnp.dot(chosen[some, :], latents[...], preferred_element_type=F32)
+            count = block // capacity
+            replies[at, pl.ds(piece * count, count)] = found.astype(BF16).reshape(
+                count, capacity, chunk
+            )
+            return carry
+        lax.fori_loop(0, slots // block, reply, 0)
+        each_peer(
+            lambda host, local, rank: rows_copy(
+                at, replies, back, send_b, recv_b, host, local, rank, me
+            ).start()
+        )
+        back[at, pl.ds(me, 1)] = replies[at, pl.ds(me, 1)]
+
+    for at in range(CHUNKS):
+        columns = slice(at * chunk, (at + 1) * chunk)
+        each_peer(
+            lambda host, local, rank: rows_copy(
+                at, replies, back, send_b, recv_b, host, local, rank, rank
+            ).wait_recv()
+        )
+        quantized[:, columns] = jnp.dot(
+            unplacing[...], back[at].reshape(slots, chunk), preferred_element_type=F32
+        ).astype(BF16)
+
+    each_peer(lambda host, local, rank: ids_copy(host, local, rank, rank).wait_send())
+    for at in range(CHUNKS):
+        each_peer(
+            lambda host, local, rank: rows_copy(
+                at, out, arrived, send_a, recv_a, host, local, rank, rank
+            ).wait_send()
+        )
+        each_peer(
+            lambda host, local, rank: rows_copy(
+                at, replies, back, send_b, recv_b, host, local, rank, rank
+            ).wait_send()
+        )
+
+
+def fused(hosts, locals_, capacity, patches, w_in, b_in, w_out, b_out, ema_sums, ema_counts, code_ids):
+    owners = hosts * locals_
+    rows, depth = patches.shape
+    span, width = ema_sums.shape
+    hidden = w_in.shape[1]
+    chunk = width // CHUNKS
+    slots = owners * capacity
+    vmem = pl.BlockSpec(memory_space=pltpu.VMEM)
+    hbm = pl.BlockSpec(memory_space=pl.ANY)
+    traded = pltpu.VMEM((CHUNKS, owners, capacity, chunk), BF16)
+    dma = pltpu.SemaphoreType.DMA
+    flops = 2 * rows * hidden * (depth + width) + 8 * slots * rows * width
+    codebook, new_counts, quantized = pl.pallas_call(
+        functools.partial(kernel, hosts, locals_, capacity),
+        out_shape=(
+            jax.ShapeDtypeStruct((span, width), F32),
+            jax.ShapeDtypeStruct((1, span), F32),
+            jax.ShapeDtypeStruct((rows, width), BF16),
+        ),
+        in_specs=[hbm, hbm, vmem, hbm, vmem, hbm, vmem, vmem],
+        out_specs=(vmem, vmem, vmem),
+        scratch_shapes=[
+            pltpu.VMEM((rows, depth), BF16),
+            pltpu.VMEM((depth, hidden), BF16),
+            pltpu.VMEM((hidden, width), BF16),
+            pltpu.VMEM((span, width), F32),
+            pltpu.VMEM((rows, hidden), BF16),
+            pltpu.VMEM((max(rows, span), chunk), BF16),
+            pltpu.VMEM((slots, rows), BF16),
+            pltpu.VMEM((rows, slots), BF16),
+            pltpu.VMEM((slots, span), BF16),
+            pltpu.VMEM((span, slots), BF16),
+            pltpu.VMEM((span, 128), F32),
+            pltpu.VMEM((owners, 8, 128), F32),
+            pltpu.VMEM((owners, 8, 128), F32),
+            traded, traded, traded, traded,
+            dma((4,)), dma((owners,)), dma((owners,)),
+            dma((CHUNKS, owners)), dma((CHUNKS, owners)),
+            dma((CHUNKS, owners)), dma((CHUNKS, owners)),
+        ],
+        compiler_params=pltpu.CompilerParams(
+            collective_id=0, has_side_effects=True, vmem_limit_bytes=60 * 2**20
+        ),
+        cost_estimate=pl.CostEstimate(
+            flops=flops, bytes_accessed=14 * 2**20, transcendentals=rows * hidden
+        ),
+    )(
+        patches, w_in, b_in.reshape(1, -1), w_out, b_out.reshape(1, -1), ema_sums,
+        ema_counts.reshape(1, -1), code_ids.reshape(1, -1),
+    )
+    return codebook, new_counts.reshape(span), quantized
+
+
+def staged(patches, w_in, b_in, w_out, b_out, ema_sums, ema_counts, code_ids):
     host_count = lax.axis_size("hst")
     local_count = lax.axis_size("local")
     owner_count = host_count * local_count
@@ -66,6 +344,18 @@
     return (codebook, new_counts, quantized)
 
 
+def per_device(patches, w_in, b_in, w_out, b_out, ema_sums, ema_counts, code_ids):
+    hosts, locals_ = lax.axis_size("hst"), lax.axis_size("local")
+    rows, span = patches.shape[0], ema_sums.shape[0]
+    capacity = max(2, 2 * rows // (hosts * locals_))
+    if capacity % 16 or 128 % capacity or rows != span:
+        return staged(patches, w_in, b_in, w_out, b_out, ema_sums, ema_counts, code_ids)
+    return fused(
+        hosts, locals_, capacity,
+        patches, w_in, b_in, w_out, b_out, ema_sums, ema_counts, code_ids,
+    )
+
+
 def solution(mesh):
     in_specs = (
         P(("hst", "local"), None),

time: 234 us -> 126 us (0.54)
  Pallas kernels: 0 us -> 120 us
  waiting for transfers between devices: 95.9 us -> 0 us
  blocking collectives: 51.6 us -> 0 us
  starting transfers between devices: 25.6 us -> 0 us
  matrix products: 22.6 us -> 0 us
  other arithmetic: 17.4 us -> 0 us
  local copies, waits for them, and re-layouts: 19.5 us -> 4.74 us
    pallas_call x0 -> x1, Pallas kernels: none -> 120 us  [fused(): pl.pallas_call(functools.partial(kernel, hosts, locals_, capacity), out_s...]
    all_to_all x5 -> x0, waiting for transfers between devices: 95.9 us -> none  [the longest x1 45.8 us: per_device(): lax.all_to_all(outgoing, 'hst', split_axis=0, concat_axis=0, tiled=True)]
    all_to_all x1 -> x0, blocking collectives: 51.6 us -> none  [per_device(): lax.all_to_all(replies, 'hst', split_axis=0, concat_axis=0, tiled=True)]
    all_to_all x5 -> x0, starting transfers between devices: 25.6 us -> none  [the longest x1 7.25 us: per_device(): lax.all_to_all(sent_ids, 'hst', split_axis=0, concat_axis=0, tiled=True)]
    dot_general x4 -> x0, matrix products: 22.6 us -> none  [the longest x1 12.1 us: per_device(): jnp.dot(hidden, w_out, preferred_element_type=jnp.float32) + b_out]
    all_to_all x6 -> x0, local copies, waits for them, and re-layouts: 10.2 us -> none  [the longest x1 3.13 us: per_device(): lax.all_to_all(outgoing, 'hst', split_axis=0, concat_axis=0, tiled=True)]
    another operation x3 -> x0, other arithmetic: 9.15 us -> none
    gather x1 -> x0, local copies, waits for them, and re-layouts: 6.98 us -> none  [per_device(): quantized = jnp.take(back_rows, slot_index, axis=0)]
  transfers between devices with their start and end apart: 5 -> 0, of which waited for: 4 -> 0; matrix products, arithmetic and copies ran while one was open for 10% -> 0% of each run, Pallas kernels for 0% -> 0%
where the time goes in v1:
time: 126 us
  Pallas kernels  120 us (95%)
  local copies, waits for them, and re-layouts  4.74 us (4%)
    pallas_call x1, Pallas kernels, fused(): pl.pallas_call(functools.partial(kernel, hosts, locals_, capacity), out_s...  120 us
    unnamed x7, local copies, waits for them, and re-layouts  4.74 us

profile of v1, /device:TPU:0, one launch (start us, length us, event | category | flops | bytes accessed | tf_op | source)
XLA Modules:
  0.0 125.8 jit_solution(7651270845089651127)
XLA Ops:
  0.6 120.4 %shard_map.103 = (f32[1024,512]{1,0:T(8,128)}, f32[1,1024]{1,0:T(1,128)}, bf16[1024,512]{1,0:T(8,128)(2,1)}) custom-call(bf16[1024,768]{1,0:T(8,128)(2,1)} %patches_hbm.1, bf16[768,3072]{1,0:T(8,128)(2,1)} %w_in_hbm.1, f32[1,3072]{1,0:T(1,128)} %bitcast.6, bf16[3072,512]{1,0:T(8,128)(2,1)} %w_out_hbm.1, f32[1,512]{1,0:T(1,128)} %bitcast.9, ...), custom_call_target="tpu_custom_call" | custom-call | flops 16642998272 | bytes 14680064 | tf_op jit(solution)/shard_map/pallas_call | solution.py:246
  121.0 0.0 copy-start.1
  121.1 0.0 copy-start
  121.1 3.2 %copy.14 = f32[1024,512]{1,0:T(8,128)} copy(f32[1024,512]{1,0:T(8,128)} %get-tuple-element.12) | data formatting | bytes 4194304
  124.2 0.0 copy-done.1
  124.2 0.6 copy.15
  124.8 0.0 copy-done
  124.8 1.0 copy.16
Async XLA Ops:
  121.0 3.2 %copy-start.1 = (f32[1,1024]{1,0:T(1,128)S(1)}, f32[1,1024]{1,0:T(1,128)}, u32[]{:S(2)}) copy-start(f32[1,1024]{1,0:T(1,128)} %get-tuple-element.7) | copy-start | bytes 12292
  121.1 3.8 %copy-start = (bf16[1024,512]{1,0:T(8,128)(2,1)S(1)}, bf16[1024,512]{1,0:T(8,128)(2,1)}, u32[]{:S(2)}) copy-start(bf16[1024,512]{1,0:T(8,128)(2,1)} %get-tuple-element.14) | copy-start | bytes 3145732

commit v2 on v1

--- a/solution.py
+++ b/solution.py
@@ -1,4 +1,5 @@
 import functools
+import math
 
 import jax
 import jax.numpy as jnp
@@ -34,10 +35,10 @@
 def kernel(
     hosts, locals_, capacity,
     patches_hbm, w_in_hbm, b_in, w_out_hbm, b_out, ema_hbm, counts_row, ids_row,
-    codebook, new_counts_row, quantized,
-    patches, w_in, w_out, ema, hidden, latents, placing, unplacing, chosen, chosen_t, scale,
+    codebook_hbm, new_counts_row, quantized,
+    codebook, patches, w_in, w_out, ema, hidden, latents, placing, unplacing, chosen, chosen_t, scale,
     ids_out, ids_in, out, arrived, replies, back,
-    load_sem, ids_send, ids_recv, send_a, recv_a, send_b, recv_b,
+    load_sem, store_sem, ids_send, ids_recv, send_a, recv_a, send_b, recv_b,
 ):
     owners = hosts * locals_
     rows = patches.shape[0]
@@ -47,19 +48,19 @@
     group = 128 // capacity
     my_host, my_local = lax.axis_index("hst"), lax.axis_index("local")
     me = my_host * locals_ + my_local
-    stride = max(1, hosts // 2 - 1)
-
-    def peer(step):
-        host = lax.rem(my_host + stride * (lax.rem(step, hosts) + 1), hosts)
-        local = lax.rem(my_local + step // hosts + 1, locals_)
-        return host, local
+    stride = next(k for k in range(max(1, hosts // 2 - 1), hosts + 1) if math.gcd(k, hosts) == 1)
 
     def each_peer(body):
-        def run(step, carry):
-            host, local = peer(step)
-            body(host, local, host * locals_ + local)
-            return carry
-        lax.fori_loop(0, owners - 1, run, 0)
+        for ahead in range(1, locals_ + 1):
+            local = my_local + ahead
+            local = jnp.where(local >= locals_, local - locals_, local)
+
+            def run(step, host):
+                host = host + stride
+                host = jnp.where(host >= hosts, host - hosts, host)
+                body(host, local, host * locals_ + local)
+                return host
+            lax.fori_loop(0, hosts - (ahead == locals_), run, my_host)
 
     loads = [
         pltpu.make_async_copy(src, dst, load_sem.at[at])
@@ -94,9 +95,8 @@
 
     code = ids - owner * span + 1
     high, low = (code // 128).astype(F32), lax.rem(code, 128).astype(F32)
-    part = lax.rem(iota((owners * 8, rows), 0), 8)
-    value = jnp.where(part == 0, high, jnp.where(part == 1, low, 0.0))
-    sending = jnp.where(iota((owners * 8, rows), 0) // 8 == owner, value, 0.0).astype(BF16)
+    line = iota((owners * 8, rows), 0) - owner * 8
+    sending = jnp.where(line == 0, high, jnp.where(line == 1, low, 0.0)).astype(BF16)
     lane = position + capacity * lax.rem(me, group)
     lanes = one_hot(iota((128, rows), 0) == lane)
     ids_out[...] = dot_nt(sending, lanes).reshape(owners, 8, 128)
@@ -109,7 +109,7 @@
     def first_layer(at, carry):
         columns = pl.ds(pl.multiple_of(at * tile, tile), tile)
         pre_act = jnp.dot(patches[...], w_in[:, columns], preferred_element_type=F32)
-        hidden[:, columns] = jnp.tanh(pre_act + b_in[:, columns]).astype(BF16)
+        hidden[:, columns] = jnp.tanh((pre_act + b_in[:, columns]).astype(BF16))
         return carry
     lax.fori_loop(0, hidden.shape[1] // tile, first_layer, 0)
     loads[2].wait()
@@ -187,7 +187,10 @@
             chosen_t[...], arrived[at].reshape(slots, chunk), preferred_element_type=F32
         )
         book = (DECAY * ema[:, columns] + (1.0 - DECAY) * sums) / scale[:, 0:1]
-        codebook[:, columns] = book
+        codebook[at] = book
+        pltpu.make_async_copy(
+            codebook.at[at], codebook_hbm.at[:, columns], store_sem.at[at]
+        ).start()
         latents[...] = book.astype(BF16)
 
         def reply(piece, carry):
@@ -218,6 +221,11 @@
         ).astype(BF16)
 
     each_peer(lambda host, local, rank: ids_copy(host, local, rank, rank).wait_send())
+    for at in range(CHUNKS):
+        columns = slice(at * chunk, (at + 1) * chunk)
+        pltpu.make_async_copy(
+            codebook.at[at], codebook_hbm.at[:, columns], store_sem.at[at]
+        ).wait()
     for at in range(CHUNKS):
         each_peer(
             lambda host, local, rank: rows_copy(
@@ -251,8 +259,9 @@
             jax.ShapeDtypeStruct((rows, width), BF16),
         ),
         in_specs=[hbm, hbm, vmem, hbm, vmem, hbm, vmem, vmem],
-        out_specs=(vmem, vmem, vmem),
+        out_specs=(hbm, vmem, vmem),
         scratch_shapes=[
+            pltpu.VMEM((CHUNKS, span, chunk), F32),
             pltpu.VMEM((rows, depth), BF16),
             pltpu.VMEM((depth, hidden), BF16),
             pltpu.VMEM((hidden, width), BF16),
@@ -267,7 +276,7 @@
             pltpu.VMEM((owners, 8, 128), F32),
             pltpu.VMEM((owners, 8, 128), F32),
             traded, traded, traded, traded,
-            dma((4,)), dma((owners,)), dma((owners,)),
+            dma((4,)), dma((CHUNKS,)), dma((owners,)), dma((owners,)),
             dma((CHUNKS, owners)), dma((CHUNKS, owners)),
             dma((CHUNKS, owners)), dma((CHUNKS, owners)),
         ],

time: 126 us -> 124 us (0.984)
    pallas_call x1, Pallas kernels: 120 us -> 119 us  [fused(): pl.pallas_call(functools.partial(kernel, hosts, locals_, capacity), out_s...]
where the time goes in v2:
time: 124 us
  Pallas kernels  119 us (96%)
  local copies, waits for them, and re-layouts  4.74 us (4%)
    pallas_call x1, Pallas kernels, fused(): pl.pallas_call(functools.partial(kernel, hosts, locals_, capacity), out_s...  119 us
    unnamed x7, local copies, waits for them, and re-layouts  4.74 us

profile of v2, /device:TPU:0, one launch (start us, length us, event | category | flops | bytes accessed | tf_op | source)
XLA Modules:
  0.0 124.0 jit_solution(8519752133884358596)
XLA Ops:
  0.6 118.6 %shard_map.103 = (f32[1024,512]{1,0:T(8,128)}, f32[1,1024]{1,0:T(1,128)}, bf16[1024,512]{1,0:T(8,128)(2,1)}) custom-call(bf16[1024,768]{1,0:T(8,128)(2,1)} %patches_hbm.1, bf16[768,3072]{1,0:T(8,128)(2,1)} %w_in_hbm.1, f32[1,3072]{1,0:T(1,128)} %bitcast.6, bf16[3072,512]{1,0:T(8,128)(2,1)} %w_out_hbm.1, f32[1,512]{1,0:T(1,128)} %bitcast.9, ...), custom_call_target="tpu_custom_call" | custom-call | flops 16642998272 | bytes 14680064 | tf_op jit(solution)/shard_map/pallas_call | solution.py:254
  119.2 0.0 copy-start.1
  119.2 0.0 copy-start
  119.2 3.2 %copy.14 = f32[1024,512]{1,0:T(8,128)} copy(f32[1024,512]{1,0:T(8,128)} %get-tuple-element.12) | data formatting | bytes 4194304
  122.4 0.0 copy-done.1
  122.4 0.6 copy.15
  123.0 0.0 copy-done
  123.0 1.0 copy.16
Async XLA Ops:
  119.2 3.2 %copy-start.1 = (f32[1,1024]{1,0:T(1,128)S(1)}, f32[1,1024]{1,0:T(1,128)}, u32[]{:S(2)}) copy-start(f32[1,1024]{1,0:T(1,128)} %get-tuple-element.7) | copy-start | bytes 12292
  119.2 3.8 %copy-start = (bf16[1024,512]{1,0:T(8,128)(2,1)S(1)}, bf16[1024,512]{1,0:T(8,128)(2,1)}, u32[]{:S(2)}) copy-start(bf16[1024,512]{1,0:T(8,128)(2,1)} %get-tuple-element.14) | copy-start | bytes 3145732

commit v3 on v2

--- a/solution.py
+++ b/solution.py
@@ -9,7 +9,8 @@
 from jax.sharding import PartitionSpec as P
 
 DECAY = 0.9
-CHUNKS = 2
+CHUNKS = 4
+DEPTH = 2
 MESH = pl.DeviceIdType.MESH
 F32 = jnp.float32
 BF16 = jnp.bfloat16
@@ -35,10 +36,10 @@
 def kernel(
     hosts, locals_, capacity,
     patches_hbm, w_in_hbm, b_in, w_out_hbm, b_out, ema_hbm, counts_row, ids_row,
-    codebook_hbm, new_counts_row, quantized,
-    codebook, patches, w_in, w_out, ema, hidden, latents, placing, unplacing, chosen, chosen_t, scale,
+    codebook, new_counts_row, quantized,
+    patches, w_in, w_out, ema, hidden, latents, placing, unplacing, chosen, chosen_t, scale,
     ids_out, ids_in, out, arrived, replies, back,
-    load_sem, store_sem, ids_send, ids_recv, send_a, recv_a, send_b, recv_b,
+    load_sem, ids_send, ids_recv, send_a, recv_a, send_b, recv_b,
 ):
     owners = hosts * locals_
     rows = patches.shape[0]
@@ -120,10 +121,26 @@
             recv_sem=ids_recv.at[slot_at], device_id=(host, local), device_id_type=MESH,
         )
 
-    def rows_copy(at, source, target, send, recv, host, local, rank, slot_at):
+    def rows_copy(turn, host, local, rank, slot_at):
+        at = turn % CHUNKS
+        source, target, send, recv = (
+            (out, arrived, send_a, recv_a) if turn < CHUNKS else (replies, back, send_b, recv_b)
+        )
         return pltpu.make_async_remote_copy(
             src_ref=source.at[at, rank], dst_ref=target.at[at, slot_at], send_sem=send.at[at, rank],
             recv_sem=recv.at[at, slot_at], device_id=(host, local), device_id_type=MESH,
+        )
+
+    def start_turn(turn):
+        def start(host, local, rank):
+            if turn >= DEPTH:
+                rows_copy(turn - DEPTH, host, local, rank, rank).wait_send()
+            rows_copy(turn, host, local, rank, me).start()
+        each_peer(start)
+
+    def wait_turn(turn):
+        each_peer(
+            lambda host, local, rank: rows_copy(turn, host, local, rank, rank).wait_recv()
         )
 
     def send_latents(at):
@@ -143,14 +160,10 @@
         if at == 0:
             pl.semaphore_wait(barrier, owners - 1)
             each_peer(lambda host, local, rank: ids_copy(host, local, rank, me).start())
-        each_peer(
-            lambda host, local, rank: rows_copy(
-                at, out, arrived, send_a, recv_a, host, local, rank, me
-            ).start()
-        )
+        start_turn(at)
         arrived[at, pl.ds(me, 1)] = out[at, pl.ds(me, 1)]
 
-    for at in range(CHUNKS):
+    for at in range(DEPTH):
         send_latents(at)
 
     for at in range(rows // 128):
@@ -176,21 +189,17 @@
         )
     loads[3].wait()
 
+    for at in range(DEPTH, CHUNKS):
+        send_latents(at)
+
     for at in range(CHUNKS):
         columns = slice(at * chunk, (at + 1) * chunk)
-        each_peer(
-            lambda host, local, rank: rows_copy(
-                at, out, arrived, send_a, recv_a, host, local, rank, rank
-            ).wait_recv()
-        )
+        wait_turn(at)
         sums = jnp.dot(
             chosen_t[...], arrived[at].reshape(slots, chunk), preferred_element_type=F32
         )
         book = (DECAY * ema[:, columns] + (1.0 - DECAY) * sums) / scale[:, 0:1]
-        codebook[at] = book
-        pltpu.make_async_copy(
-            codebook.at[at], codebook_hbm.at[:, columns], store_sem.at[at]
-        ).start()
+        codebook[:, columns] = book
         latents[...] = book.astype(BF16)
 
         def reply(piece, carry):
@@ -202,40 +211,20 @@
             )
             return carry
         lax.fori_loop(0, slots // block, reply, 0)
-        each_peer(
-            lambda host, local, rank: rows_copy(
-                at, replies, back, send_b, recv_b, host, local, rank, me
-            ).start()
-        )
+        start_turn(CHUNKS + at)
         back[at, pl.ds(me, 1)] = replies[at, pl.ds(me, 1)]
 
     for at in range(CHUNKS):
         columns = slice(at * chunk, (at + 1) * chunk)
-        each_peer(
-            lambda host, local, rank: rows_copy(
-                at, replies, back, send_b, recv_b, host, local, rank, rank
-            ).wait_recv()
-        )
+        wait_turn(CHUNKS + at)
         quantized[:, columns] = jnp.dot(
             unplacing[...], back[at].reshape(slots, chunk), preferred_element_type=F32
         ).astype(BF16)
 
     each_peer(lambda host, local, rank: ids_copy(host, local, rank, rank).wait_send())
-    for at in range(CHUNKS):
-        columns = slice(at * chunk, (at + 1) * chunk)
-        pltpu.make_async_copy(
-            codebook.at[at], codebook_hbm.at[:, columns], store_sem.at[at]
-        ).wait()
-    for at in range(CHUNKS):
+    for turn in range(2 * CHUNKS - DEPTH, 2 * CHUNKS):
         each_peer(
-            lambda host, local, rank: rows_copy(
-                at, out, arrived, send_a, recv_a, host, local, rank, rank
-            ).wait_send()
-        )
-        each_peer(
-            lambda host, local, rank: rows_copy(
-                at, replies, back, send_b, recv_b, host, local, rank, rank
-            ).wait_send()
+            lambda host, local, rank: rows_copy(turn, host, local, rank, rank).wait_send()
         )
 
 
@@ -254,14 +243,13 @@
     codebook, new_counts, quantized = pl.pallas_call(
         functools.partial(kernel, hosts, locals_, capacity),
         out_shape=(
-            jax.ShapeDtypeStruct((span, width), F32),
+            pltpu.VMEM((span, width), F32),
             jax.ShapeDtypeStruct((1, span), F32),
-            jax.ShapeDtypeStruct((rows, width), BF16),
+            pltpu.VMEM((rows, width), BF16),
         ),
         in_specs=[hbm, hbm, vmem, hbm, vmem, hbm, vmem, vmem],
-        out_specs=(hbm, vmem, vmem),
+        out_specs=(vmem, vmem, vmem),
         scratch_shapes=[
-            pltpu.VMEM((CHUNKS, span, chunk), F32),
             pltpu.VMEM((rows, depth), BF16),
             pltpu.VMEM((depth, hidden), BF16),
             pltpu.VMEM((hidden, width), BF16),
@@ -276,12 +264,12 @@
             pltpu.VMEM((owners, 8, 128), F32),
             pltpu.VMEM((owners, 8, 128), F32),
             traded, traded, traded, traded,
-            dma((4,)), dma((CHUNKS,)), dma((owners,)), dma((owners,)),
+            dma((4,)), dma((owners,)), dma((owners,)),
             dma((CHUNKS, owners)), dma((CHUNKS, owners)),
             dma((CHUNKS, owners)), dma((CHUNKS, owners)),
         ],
         compiler_params=pltpu.CompilerParams(
-            collective_id=0, has_side_effects=True, vmem_limit_bytes=60 * 2**20
+            collective_id=0, has_side_effects=True, vmem_limit_bytes=56 * 2**20
         ),
         cost_estimate=pl.CostEstimate(
             flops=flops, bytes_accessed=14 * 2**20, transcendentals=rows * hidden

time: 124 us -> 124 us (level)
  local copies, waits for them, and re-layouts: 4.74 us -> 2.89 us
    pallas_call x1, Pallas kernels: 119 us -> 120 us  [fused(): pl.pallas_call(functools.partial(kernel, hosts, locals_, capacity), out_s...]
    unnamed x7 -> x5, local copies, waits for them, and re-layouts: 4.74 us -> 2.89 us
where the time goes in v3:
time: 124 us
  Pallas kernels  120 us (97%)
  local copies, waits for them, and re-layouts  2.89 us (2%)
    pallas_call x1, Pallas kernels, fused(): pl.pallas_call(functools.partial(kernel, hosts, locals_, capacity), out_s...  120 us
    unnamed x5, local copies, waits for them, and re-layouts  2.89 us

profile of v3, /device:TPU:0, one launch (start us, length us, event | category | flops | bytes accessed | tf_op | source)
XLA Modules:
  0.0 124.0 jit_solution(6639228917241193075)
XLA Ops:
  0.6 120.4 %shard_map.103 = (f32[1024,512]{1,0:T(8,128)S(1)}, f32[1,1024]{1,0:T(1,128)}, bf16[1024,512]{1,0:T(8,128)(2,1)S(1)}) custom-call(bf16[1024,768]{1,0:T(8,128)(2,1)} %patches_hbm.1, bf16[768,3072]{1,0:T(8,128)(2,1)} %w_in_hbm.1, f32[1,3072]{1,0:T(1,128)} %bitcast.6, bf16[3072,512]{1,0:T(8,128)(2,1)} %w_out_hbm.1, f32[1,512]{1,0:T(1,128)} %bitcast.9, ...), custom_call_target="tpu_custom_call" | custom-call | flops 16642998272 | bytes 14680064 | tf_op jit(solution)/shard_map/pallas_call | solution.py:243
  121.1 1.3 %copy.14 = f32[1024,512]{1,0:T(8,128)} copy(f32[1024,512]{1,0:T(8,128)S(1)} %get-tuple-element.9) | data formatting | bytes 4194304
  122.4 0.0 copy-start
  122.4 1.0 copy.15
  123.4 0.0 copy-done
  123.4 0.6 copy.16
Async XLA Ops:
  122.4 1.0 copy-start

commit v4 on v3

--- a/solution.py
+++ b/solution.py
@@ -9,7 +9,7 @@
 from jax.sharding import PartitionSpec as P
 
 DECAY = 0.9
-CHUNKS = 4
+CHUNKS = 2
 DEPTH = 2
 MESH = pl.DeviceIdType.MESH
 F32 = jnp.float32
@@ -86,13 +86,7 @@
     position = jnp.sum(jnp.where(members, running, 0.0), axis=0, keepdims=True) - 1.0
     position = position.astype(jnp.int32)
     slot = owner * capacity + position
-    block = min(slots, 256)
-
-    def fill_placing(at, carry):
-        start = pl.multiple_of(at * block, block)
-        placing[pl.ds(start, block), :] = one_hot(iota((block, rows), 0) + start == slot)
-        return carry
-    lax.fori_loop(0, slots // block, fill_placing, 0)
+    block = min(slots, 512)
 
     code = ids - owner * span + 1
     high, low = (code // 128).astype(F32), lax.rem(code, 128).astype(F32)
@@ -105,14 +99,17 @@
 
     loads[0].wait()
     loads[1].wait()
-    tile = 512
+    steps = slots // block
+    tile = hidden.shape[1] // steps
 
     def first_layer(at, carry):
         columns = pl.ds(pl.multiple_of(at * tile, tile), tile)
         pre_act = jnp.dot(patches[...], w_in[:, columns], preferred_element_type=F32)
+        start = pl.multiple_of(at * block, block)
+        placing[pl.ds(start, block), :] = one_hot(iota((block, rows), 0) + start == slot)
         hidden[:, columns] = jnp.tanh((pre_act + b_in[:, columns]).astype(BF16))
         return carry
-    lax.fori_loop(0, hidden.shape[1] // tile, first_layer, 0)
+    lax.fori_loop(0, steps, first_layer, 0)
     loads[2].wait()
 
     def ids_copy(host, local, rank, slot_at):
@@ -159,8 +156,9 @@
         lax.fori_loop(0, slots // block, pack, 0)
         if at == 0:
             pl.semaphore_wait(barrier, owners - 1)
+        start_turn(at)
+        if at == 0:
             each_peer(lambda host, local, rank: ids_copy(host, local, rank, me).start())
-        start_turn(at)
         arrived[at, pl.ds(me, 1)] = out[at, pl.ds(me, 1)]
 
     for at in range(DEPTH):
@@ -216,16 +214,16 @@
 
     for at in range(CHUNKS):
         columns = slice(at * chunk, (at + 1) * chunk)
+        if at == CHUNKS - 1:
+            each_peer(lambda host, local, rank: ids_copy(host, local, rank, rank).wait_send())
+            for turn in range(2 * CHUNKS - DEPTH, 2 * CHUNKS):
+                each_peer(
+                    lambda host, local, rank: rows_copy(turn, host, local, rank, rank).wait_send()
+                )
         wait_turn(CHUNKS + at)
         quantized[:, columns] = jnp.dot(
             unplacing[...], back[at].reshape(slots, chunk), preferred_element_type=F32
         ).astype(BF16)
-
-    each_peer(lambda host, local, rank: ids_copy(host, local, rank, rank).wait_send())
-    for turn in range(2 * CHUNKS - DEPTH, 2 * CHUNKS):
-        each_peer(
-            lambda host, local, rank: rows_copy(turn, host, local, rank, rank).wait_send()
-        )
 
 
 def fused(hosts, locals_, capacity, patches, w_in, b_in, w_out, b_out, ema_sums, ema_counts, code_ids):
@@ -345,7 +343,8 @@
     hosts, locals_ = lax.axis_size("hst"), lax.axis_size("local")
     rows, span = patches.shape[0], ema_sums.shape[0]
     capacity = max(2, 2 * rows // (hosts * locals_))
-    if capacity % 16 or 128 % capacity or rows != span:
+    slots = hosts * locals_ * capacity
+    if capacity % 16 or 128 % capacity or rows != span or slots % 512:
         return staged(patches, w_in, b_in, w_out, b_out, ema_sums, ema_counts, code_ids)
     return fused(
         hosts, locals_, capacity,

time: 124 us -> 120 us (0.968)
  Pallas kernels: 120 us -> 116 us
    pallas_call x1, Pallas kernels: 120 us -> 116 us  [fused(): pl.pallas_call(functools.partial(kernel, hosts, locals_, capacity), out_s...]
where the time goes in v4:
time: 120 us
  Pallas kernels  116 us (97%)
  local copies, waits for them, and re-layouts  2.89 us (2%)
    pallas_call x1, Pallas kernels, fused(): pl.pallas_call(functools.partial(kernel, hosts, locals_, capacity), out_s...  116 us
    unnamed x5, local copies, waits for them, and re-layouts  2.89 us

profile of v4, /device:TPU:0, one launch (start us, length us, event | category | flops | bytes accessed | tf_op | source)
XLA Modules:
  0.0 119.6 jit_solution(18185602683405447306)
XLA Ops:
  0.6 116.1 %shard_map.103 = (f32[1024,512]{1,0:T(8,128)S(1)}, f32[1,1024]{1,0:T(1,128)}, bf16[1024,512]{1,0:T(8,128)(2,1)S(1)}) custom-call(bf16[1024,768]{1,0:T(8,128)(2,1)} %patches_hbm.1, bf16[768,3072]{1,0:T(8,128)(2,1)} %w_in_hbm.1, f32[1,3072]{1,0:T(1,128)} %bitcast.6, bf16[3072,512]{1,0:T(8,128)(2,1)} %w_out_hbm.1, f32[1,512]{1,0:T(1,128)} %bitcast.9, ...), custom_call_target="tpu_custom_call" | custom-call | flops 16642998272 | bytes 14680064 | tf_op jit(solution)/shard_map/pallas_call | solution.py:241
  116.7 1.3 %copy.14 = f32[1024,512]{1,0:T(8,128)} copy(f32[1024,512]{1,0:T(8,128)S(1)} %get-tuple-element.9) | data formatting | bytes 4194304
  118.0 0.0 copy-start
  118.0 1.0 copy.15
  119.0 0.0 copy-done
  119.0 0.6 copy.16
Async XLA Ops:
  118.0 1.0 copy-start

commit v5 on v4

--- a/solution.py
+++ b/solution.py
@@ -88,15 +88,6 @@
     slot = owner * capacity + position
     block = min(slots, 512)
 
-    code = ids - owner * span + 1
-    high, low = (code // 128).astype(F32), lax.rem(code, 128).astype(F32)
-    line = iota((owners * 8, rows), 0) - owner * 8
-    sending = jnp.where(line == 0, high, jnp.where(line == 1, low, 0.0)).astype(BF16)
-    lane = position + capacity * lax.rem(me, group)
-    lanes = one_hot(iota((128, rows), 0) == lane)
-    ids_out[...] = dot_nt(sending, lanes).reshape(owners, 8, 128)
-    ids_in[pl.ds(me, 1)] = ids_out[pl.ds(me, 1)]
-
     loads[0].wait()
     loads[1].wait()
     steps = slots // block
@@ -111,6 +102,16 @@
         return carry
     lax.fori_loop(0, steps, first_layer, 0)
     loads[2].wait()
+
+    def pack_ids():
+        code = ids - owner * span + 1
+        high, low = (code // 128).astype(F32), lax.rem(code, 128).astype(F32)
+        line = iota((owners * 8, rows), 0) - owner * 8
+        sending = jnp.where(line == 0, high, jnp.where(line == 1, low, 0.0)).astype(BF16)
+        lane = position + capacity * lax.rem(me, group)
+        lanes = one_hot(iota((128, rows), 0) == lane)
+        ids_out[...] = dot_nt(sending, lanes).reshape(owners, 8, 128)
+        ids_in[pl.ds(me, 1)] = ids_out[pl.ds(me, 1)]
 
     def ids_copy(host, local, rank, slot_at):
         return pltpu.make_async_remote_copy(
@@ -158,6 +159,7 @@
             pl.semaphore_wait(barrier, owners - 1)
         start_turn(at)
         if at == 0:
+            pack_ids()
             each_peer(lambda host, local, rank: ids_copy(host, local, rank, me).start())
         arrived[at, pl.ds(me, 1)] = out[at, pl.ds(me, 1)]
 

time: 120 us -> 120 us (level)
  no operation moved by 1% of the time
where the time goes in v5:
time: 120 us
  Pallas kernels  116 us (97%)
  local copies, waits for them, and re-layouts  2.89 us (2%)
    pallas_call x1, Pallas kernels, fused(): pl.pallas_call(functools.partial(kernel, hosts, locals_, capacity), out_s...  116 us
    unnamed x5, local copies, waits for them, and re-layouts  2.89 us

profile of v5, /device:TPU:0, one launch (start us, length us, event | category | flops | bytes accessed | tf_op | source)
XLA Modules:
  0.0 119.6 jit_solution(9322381153326060790)
XLA Ops:
  0.6 116.0 %shard_map.103 = (f32[1024,512]{1,0:T(8,128)S(1)}, f32[1,1024]{1,0:T(1,128)}, bf16[1024,512]{1,0:T(8,128)(2,1)S(1)}) custom-call(bf16[1024,768]{1,0:T(8,128)(2,1)} %patches_hbm.1, bf16[768,3072]{1,0:T(8,128)(2,1)} %w_in_hbm.1, f32[1,3072]{1,0:T(1,128)} %bitcast.6, bf16[3072,512]{1,0:T(8,128)(2,1)} %w_out_hbm.1, f32[1,512]{1,0:T(1,128)} %bitcast.9, ...), custom_call_target="tpu_custom_call" | custom-call | flops 16642998272 | bytes 14680064 | tf_op jit(solution)/shard_map/pallas_call | solution.py:243
  116.7 1.3 %copy.14 = f32[1024,512]{1,0:T(8,128)} copy(f32[1024,512]{1,0:T(8,128)S(1)} %get-tuple-element.9) | data formatting | bytes 4194304
  118.0 0.0 copy-start
  118.0 1.0 copy.15
  119.0 0.0 copy-done
  119.0 0.6 copy.16
Async XLA Ops:
  118.0 1.0 copy-start
